TPU v7x, 512 devices: a whole 4x8x8 slice. The times are simulated.
512 devices in a mesh: wide: 64 (over z, y_hi, core), narrow: 8 (over y_lo, x).
Axes of the slice: x: 4, y: 8 (y_hi: 4, y_lo: 2; y = y_hi * 2 + y_lo), z: 8, core: 2. Of those that a mesh axis runs over, the one named last changes fastest.
Arguments:
- fields: float32 [5, 192, 64, 1024], P(None, 'wide', 'narrow'), may hold values from -6 to 6
- y_bands: float32 [3, 192], replicated, may hold values from -1.5 to 4, as said below
Outputs:
- new_fields: float32 [5, 192, 64, 1024], P(None, 'wide', 'narrow')
- pressure: float32 [192, 64, 1024], P('wide', 'narrow')
Inputs may be any that keep to these rules, and one draw needn't show every extreme that they name: `y_bands`: row 0 holds the couplings to the row below (its first entry zero), row 1 the diagonal, row 2 the couplings to the row above (its last entry zero); the matrix is symmetric and each diagonal entry exceeds the sum of the magnitudes beside it.
All inputs are finite; a program needn't handle non-finite values.
Results may differ from a plain program's by a relative error of at most 0.0003.
Values sent between devices are 32-bit elements; how exact they have to be, the bound alone decides.
A program may use at most 128 MiB of HBM per device.

v0:
```python
import functools
import math

import jax
import jax.numpy as jnp
import ml_dtypes
import numpy as np
from jax import lax
from jax.experimental import pallas as pl
from jax.experimental.pallas import tpu as pltpu
from jax.sharding import PartitionSpec as P

EPSILON = 1e-06
STEP = 0.05
GRAVITY = 0.5
MOLECULAR = [0.02, 0.02, 0.02, 0.028, 0.04]
TURBULENT = [1.0, 1.0, 1.0, 1.0 / 0.85, 1.0 / 0.7]
PAIRS = [(0, 0), (1, 1), (2, 2), (0, 1), (0, 2), (1, 2)]
LANES = 128
SUBS = 8
CY = 3
ZB = 8


def basis(count):
    half = count // 2
    modes = np.arange(count)
    wave = np.where(modes <= half, modes, modes - half)
    phase = (wave[:, None] * np.arange(count)[None, :]) % count
    angle = 2.0 * math.pi / count * phase
    table = np.where(modes[:, None] <= half, np.cos(angle), np.sin(angle))
    weight = np.where((modes == 0) | (modes == half), 1.0, 2.0) / count
    lam = 2.0 - 2.0 * np.cos(2.0 * math.pi / count * wave)
    return table, weight, lam


def split_table(table):
    high = table.astype(ml_dtypes.bfloat16)
    low = (table - high.astype(np.float64)).astype(ml_dtypes.bfloat16)
    return high, low


@functools.lru_cache
def tables(length_x, span_all, wide, narrow):
    basis_x, weight_x, lam_x = basis(length_x)
    basis_z, weight_z, lam_z = basis(span_all)
    forward = split_table(basis_x.T)
    inverse = split_table(basis_x)
    rows = np.zeros((2 * narrow + 2 * wide, LANES), np.float32)
    rows[0:narrow] = lam_x.reshape(narrow, LANES)
    rows[narrow : 2 * narrow] = weight_x.reshape(narrow, LANES)
    rows[2 * narrow : 2 * narrow + wide] = lam_z[:, None]
    rows[2 * narrow + wide :] = weight_z[:, None]
    zmat = np.zeros((span_all, 512), np.float32)
    zmat[:, 0:span_all] = basis_z
    zmat[:, 128 : 128 + span_all] = basis_z.T
    for n in range(narrow):
        for y in range(CY):
            for side in range(2):
                z = (ZB * n - 1 if side == 0 else ZB * n + ZB) % span_all
                row = ZB * n + 2 * y + side
                zmat[row, 256 + y * span_all : 256 + (y + 1) * span_all] = basis_z[:, z]
    return (*forward, *inverse, rows, zmat)


def shift_x(value, step):
    lane = lax.broadcasted_iota(jnp.int32, value.shape, value.ndim - 1)
    if step > 0:
        moved = pltpu.roll(value, LANES - step, value.ndim - 1)
        carried = pltpu.roll(moved, SUBS - 1, value.ndim - 2)
        return jnp.where(lane >= LANES - step, carried, moved)
    moved = pltpu.roll(value, -step, value.ndim - 1)
    carried = pltpu.roll(moved, 1, value.ndim - 2)
    return jnp.where(lane < -step, carried, moved)


def three(below, centre, above):
    return (below + above) + (centre + centre)


def filter_x(value):
    return three(shift_x(value, -1), value, shift_x(value, 1)) * (1.0 / 64.0)


def strain(at, y, z):
    grads = []
    for i in range(3):
        here = at(i, y, z)
        grads.append(
            (
                shift_x(here, 1) - shift_x(here, -1),
                at(i, y + 1, z) - at(i, y - 1, z),
                at(i, y, z + 1) - at(i, y, z - 1),
            )
        )
    parts = [
        grads[i][i] if i == j else 0.5 * (grads[i][j] + grads[j][i]) for i, j in PAIRS
    ]
    diag = parts[0] * parts[0] + parts[1] * parts[1] + parts[2] * parts[2]
    off = parts[3] * parts[3] + parts[4] * parts[4] + parts[5] * parts[5]
    return parts, jnp.sqrt(0.5 * diag + off)


def shift_rows(value, step, filler):
    pad = jnp.full((abs(step), value.shape[1]), filler, value.dtype)
    if step > 0:
        return jnp.concatenate([pad, value[: value.shape[0] - step]], 0)
    return jnp.concatenate([value[-step:], pad], 0)


def exact_dot(left, right):
    return jnp.dot(
        left, right, precision=lax.Precision.HIGHEST, preferred_element_type=jnp.float32
    )


def split_dot(rows, high_ref, low_ref):
    count = rows.shape[0]
    high = rows.astype(jnp.bfloat16)
    low = (rows - high.astype(jnp.float32)).astype(jnp.bfloat16)
    both = jnp.dot(
        jnp.concatenate([high, low], 0), high_ref[...], preferred_element_type=jnp.float32
    )
    rest = jnp.dot(high, low_ref[...], preferred_element_type=jnp.float32)
    return both[:count] + (both[count:] + rest)


def kernel(
    wide,
    narrow,
    fields_hbm,
    bands_ref,
    fhigh_hbm,
    flow_hbm,
    ihigh_hbm,
    ilow_hbm,
    rows_hbm,
    zmat_hbm,
    out_ref,
    press_ref,
    nat,
    fhigh,
    flow,
    ihigh,
    ilow,
    rowtab,
    zmat,
    pad,
    yfilt,
    ymod,
    yprod,
    mag,
    filt,
    part_a,
    part_b,
    pred,
    div,
    sums,
    mine,
    factors,
    final,
    n_send,
    n_recv,
    w_send,
    w_recv,
    v_send,
    v_recv,
    u_send,
    u_recv,
    local_sem,
    halo_send,
    halo_recv,
    phase_send,
    phase_recv,
):
    w = lax.axis_index("wide")
    n = lax.axis_index("narrow")
    height = wide * CY
    w_down, w_up = lax.rem(w + wide - 1, wide), lax.rem(w + 1, wide)
    n_down, n_up = lax.rem(n + narrow - 1, narrow), lax.rem(n + 1, narrow)

    locals_ = [
        pltpu.make_async_copy(src, dst, local_sem.at[k])
        for k, (src, dst) in enumerate(
            [
                (fields_hbm, nat),
                (rows_hbm, rowtab),
                (zmat_hbm, zmat),
                (fhigh_hbm, fhigh),
                (flow_hbm, flow),
                (ihigh_hbm, ihigh),
                (ilow_hbm, ilow),
            ]
        )
    ]
    for copy in locals_:
        copy.start()

    barrier = pltpu.get_barrier_semaphore()

    def greet(to_w, to_n):
        pl.semaphore_signal(
            barrier,
            inc=1,
            device_id={"wide": to_w, "narrow": to_n},
            device_id_type=pl.DeviceIdType.MESH,
        )

    def greet_wide(d, carry):
        greet(lax.rem(w + d, wide), n)
        return carry

    for d in range(1, narrow):
        to_n = lax.rem(n + d, narrow)
        greet(w_down, to_n)
        greet(w_up, to_n)
        greet(w, to_n)
    lax.fori_loop(1, wide, greet_wide, 0)

    def remote(src, dst, send, recv, to_w, to_n):
        return pltpu.make_async_remote_copy(
            src_ref=src,
            dst_ref=dst,
            send_sem=send,
            recv_sem=recv,
            device_id={"wide": to_w, "narrow": to_n},
            device_id_type=pl.DeviceIdType.MESH,
        )

    locals_[0].wait()

    def to_tiles(f, carry):
        for y in range(CY):
            for z in range(ZB):
                pad[f, y + 3, z + 3] = nat[pl.ds((f * CY + y) * 64 + z, SUBS, stride=ZB), :]
        return carry

    lax.fori_loop(0, 5, to_tiles, 0)

    pl.semaphore_wait(barrier, (wide - 1) + 3 * (narrow - 1))

    def both(fs, ys, zs):
        return pad.at[pl.ds(*fs), pl.ds(*ys), pl.ds(*zs)]

    own_z = (3, ZB)
    own_y = (3, CY)
    vel, sca = (0, 3), (3, 2)
    plan = [
        (vel, (3, 2), own_z, (6, 2), own_z, w_down, n),
        (vel, (4, 2), own_z, (1, 2), own_z, w_up, n),
        (vel, (3, 2), (3, 2), (6, 2), (11, 2), w_down, n_down),
        (vel, (3, 2), (9, 2), (6, 2), (1, 2), w_down, n_up),
        (vel, (4, 2), (3, 2), (1, 2), (11, 2), w_up, n_down),
        (vel, (4, 2), (9, 2), (1, 2), (1, 2), w_up, n_up),
        (vel, own_y, (3, 2), own_y, (11, 2), w, n_down),
        (vel, own_y, (9, 2), own_y, (1, 2), w, n_up),
        (sca, (3, 2), own_z, (6, 2), own_z, w_down, n),
        (sca, (4, 2), own_z, (1, 2), own_z, w_up, n),
        (sca, own_y, (3, 2), own_y, (11, 2), w, n_down),
        (sca, own_y, (9, 2), own_y, (1, 2), w, n_up),
        ((1, 1), (5, 1), own_z, (8, 1), own_z, w_down, n),
        ((1, 1), (3, 1), own_z, (0, 1), own_z, w_up, n),
        ((2, 1), own_y, (5, 1), own_y, (13, 1), w, n_down),
        ((2, 1), own_y, (8, 1), own_y, (0, 1), w, n_up),
    ]
    halos = []
    for k, (fs, sy, sz, ty, tz, to_w, to_n) in enumerate(plan):
        halos.append(
            remote(
                both(fs, sy, sz), both(fs, ty, tz), halo_send.at[k], halo_recv.at[k], to_w, to_n
            )
        )
        halos[-1].start()

    locals_[1].wait()
    band = lax.broadcasted_iota(jnp.int32, (3, LANES), 0)
    spread = [
        lax.dot_general(
            bands_ref[...],
            jnp.where(band == k, 1.0, 0.0).astype(jnp.float32),
            (((0,), (0,)), ((), ())),
            precision=lax.Precision.HIGHEST,
            preferred_element_type=jnp.float32,
        )
        for k in range(3)
    ]
    eig = rowtab[pl.ds(n, 1), :] + rowtab[pl.ds(2 * narrow + w, 1), :]
    lower, diag, upper = spread[0], spread[1] + eig, spread[2]
    stride = 1
    level = 0
    while stride < height:
        inv = 1.0 / diag
        low = -lower * shift_rows(inv, stride, 1.0)
        high = -upper * shift_rows(inv, -stride, 1.0)
        factors[level, 0] = low
        factors[level, 1] = high
        diag = (
            diag
            + low * shift_rows(upper, stride, 0.0)
            + high * shift_rows(lower, -stride, 0.0)
        )
        lower = low * shift_rows(lower, stride, 0.0)
        upper = high * shift_rows(upper, -stride, 0.0)
        stride *= 2
        level += 1
    weight = rowtab[pl.ds(narrow + n, 1), :] * rowtab[pl.ds(2 * narrow + wide + w, 1), :]
    final[...] = -weight / diag

    for k in range(8):
        halos[k].wait_recv()

    def clear(start, fields, first):
        def one(z, carry):
            for f in range(fields[0], fields[0] + fields[1]):
                for y in range(first, first + start):
                    pad[f, y, z] = jnp.zeros((SUBS, LANES), jnp.float32)
            return carry

        lax.fori_loop(0, ZB + 6, one, 0)

    @pl.when(w == 0)
    def _():
        clear(2, vel, 1)

    @pl.when(w == wide - 1)
    def _():
        clear(2, vel, 6)

    def at_pad(f, y, z):
        return pad[f, y + 3, z + 3]

    def filter_rows(iz, carry):
        z = iz - 2
        for i in range(3):
            column = [at_pad(i, y, z) for y in range(-2, 5)]
            for y in range(5):
                yfilt[i, y, iz] = three(column[y], column[y + 1], column[y + 2])
        return carry

    lax.fori_loop(0, ZB + 4, filter_rows, 0)

    def local_terms(iz, carry):
        z = iz - 1
        modeled = []
        for y in range(-1, 4):
            parts, size = strain(at_pad, y, z)
            mag[y + 1, iz] = size
            modeled.append([size * part for part in parts])
        for p in range(6):
            for y in range(CY):
                ymod[p, y, iz] = three(modeled[y][p], modeled[y + 1][p], modeled[y + 2][p])
        columns = [[at_pad(i, y, z) for y in range(-1, 4)] for i in range(3)]
        for p, (i, j) in enumerate(PAIRS):
            prods = [columns[i][y] * columns[j][y] for y in range(5)]
            for y in range(CY):
                yprod[p, y, iz] = three(prods[y], prods[y + 1], prods[y + 2])
        for i in range(3):
            for y in range(5):
                value = three(yfilt[i, y, iz], yfilt[i, y, iz + 1], yfilt[i, y, iz + 2])
                filt[i, y, iz] = filter_x(value)
        return carry

    lax.fori_loop(0, ZB + 2, local_terms, 0)

    def at_filt(f, y, z):
        return filt[f, y + 1, z + 1]

    def plane_terms(z, carry):
        cross, square = list(carry[0]), list(carry[1])
        for y in range(CY):
            parts, size = strain(at_filt, y, z)
            centre = [at_filt(i, y, z) for i in range(3)]
            four = 4.0 * size
            lm_diag = lm_off = mm_diag = mm_off = None
            for p, (i, j) in enumerate(PAIRS):
                model = filter_x(three(ymod[p, y, z], ymod[p, y, z + 1], ymod[p, y, z + 2]))
                model = model - four * parts[p]
                stress = filter_x(three(yprod[p, y, z], yprod[p, y, z + 1], yprod[p, y, z + 2]))
                stress = stress - centre[i] * centre[j]
                if p < 3:
                    lm_diag = stress * model if lm_diag is None else lm_diag + stress * model
                    mm_diag = model * model if mm_diag is None else mm_diag + model * model
                else:
                    lm_off = stress * model if lm_off is None else lm_off + stress * model
                    mm_off = model * model if mm_off is None else mm_off + model * model
            cross[y] = cross[y] + (lm_diag + (lm_off + lm_off))
            square[y] = square[y] + (mm_diag + (mm_off + mm_off))
        return tuple(cross), tuple(square)

    nothing = jnp.zeros((SUBS, LANES), jnp.float32)
    cross, square = lax.fori_loop(
        0, ZB, plane_terms, ((nothing,) * CY, (nothing,) * CY)
    )
    packed = [jnp.sum(v, 0, keepdims=True) for v in (*cross, *square)]
    packed.append(jnp.zeros((SUBS - 2 * CY, LANES), jnp.float32))
    tile = jnp.concatenate(packed, 0)
    tile = jnp.broadcast_to(jnp.sum(tile, 1, keepdims=True), (SUBS, LANES))
    mine[...] = tile
    sums[pl.ds(narrow + n, 1)] = tile[None]
    peers = [(w_down, 2), (w, 1), (w_up, 0)]
    for d in range(narrow):
        to_n = lax.rem(n + d, narrow)
        for to_w, slot in peers:
            if d == 0 and slot == 1:
                continue
            remote(
                mine,
                sums.at[slot * narrow + n],
                phase_send.at[0],
                phase_recv.at[0],
                to_w,
                to_n,
            ).start()

    for k in range(8, 16):
        halos[k].wait_recv()

    @pl.when(w == 0)
    def _():
        clear(2, sca, 1)
        clear(1, (1, 1), 0)

    @pl.when(w == wide - 1)
    def _():
        clear(2, sca, 6)
        clear(1, (1, 1), 8)

    def slot_of(f, y, z):
        return pl.ds(pl.multiple_of(((f * 5 + y + 1) * (ZB + 2) + z + 1) * SUBS, SUBS), SUBS)

    def advance(fs, y, z):
        velocity = [at_pad(i, y, z) for i in range(3)]
        size = mag[y + 1, z + 1]
        for f in fs:
            here = velocity[f] if f < 3 else at_pad(f, y, z)
            xp, xm = shift_x(here, 1), shift_x(here, -1)
            yp, ym = at_pad(f, y + 1, z), at_pad(f, y - 1, z)
            zp, zm = at_pad(f, y, z + 1), at_pad(f, y, z - 1)
            ex = 8.0 * (xp - xm) - (shift_x(here, 2) - shift_x(here, -2))
            ey = 8.0 * (yp - ym) - (at_pad(f, y + 2, z) - at_pad(f, y - 2, z))
            ez = 8.0 * (zp - zm) - (at_pad(f, y, z + 2) - at_pad(f, y, z - 2))
            carried = velocity[0] * ex + velocity[1] * ey + velocity[2] * ez
            lap = ((xp + xm) + (yp + ym)) + ((zp + zm) - 6.0 * here)
            value = here - (STEP / 12.0) * carried + (STEP * MOLECULAR[f]) * lap
            if f == 1:
                value = value + (STEP * GRAVITY) * at_pad(3, y, z)
            part_a[slot_of(f, y, z), :] = value
            part_b[slot_of(f, y, z), :] = (STEP * TURBULENT[f]) * (size * lap)

    def advance_cells(z, carry):
        for y in range(CY):
            advance(range(5), y, z)
        advance((1,), -1, z)
        advance((1,), CY, z)
        return carry

    lax.fori_loop(0, ZB, advance_cells, 0)
    for y in range(CY):
        advance((2,), y, -1)
        advance((2,), y, ZB)

    pltpu.make_async_copy(
        sums.at[pl.ds(0, 3 * narrow - 1)], sums.at[pl.ds(0, 3 * narrow - 1)], phase_recv.at[0]
    ).wait()
    coef = []
    for slot, rows in ((0, (2,)), (1, (0, 1, 2)), (2, (0,))):
        total = sums[slot * narrow]
        for k in range(1, narrow):
            total = total + sums[slot * narrow + k]
        for row in rows:
            ratio = total[row : row + 1] / (total[CY + row : CY + row + 1] + EPSILON)
            coef.append(jnp.broadcast_to(ratio, (SUBS, LANES)))

    def finish(f, y, z, scale=None):
        value = part_a[slot_of(f, y, z), :] + coef[y + 1] * part_b[slot_of(f, y, z), :]
        pred[slot_of(f, y, z), :] = value if scale is None else value * scale

    inside_low = jnp.where(w == 0, 0.0, 1.0)
    inside_high = jnp.where(w == wide - 1, 0.0, 1.0)

    def finish_cells(z, carry):
        for y in range(CY):
            for f in range(5):
                finish(f, y, z)
        finish(1, -1, z, inside_low)
        finish(1, CY, z, inside_high)
        return carry

    lax.fori_loop(0, ZB, finish_cells, 0)
    for y in range(CY):
        finish(2, y, -1)
        finish(2, y, ZB)

    def at_pred(f, y, z):
        return pred[slot_of(f, y, z), :]

    def divergence(z, carry):
        for y in range(CY):
            stream = at_pred(0, y, z)
            value = shift_x(stream, 1) - shift_x(stream, -1)
            value = value + (at_pred(1, y + 1, z) - at_pred(1, y - 1, z))
            value = value + (at_pred(2, y, z + 1) - at_pred(2, y, z - 1))
            div[pl.ds(pl.multiple_of((y * ZB + z) * SUBS, SUBS), SUBS), :] = 0.5 * value
        return carry

    lax.fori_loop(0, ZB, divergence, 0)

    locals_[3].wait()
    locals_[4].wait()
    flat = jnp.concatenate(
        [div[pl.ds(s, CY * ZB, stride=SUBS), :] for s in range(SUBS)], 1
    )
    flat = jnp.concatenate([flat, jnp.zeros((8, flat.shape[1]), jnp.float32)], 0)
    spectrum = split_dot(flat, fhigh, flow)
    for k in range(narrow):
        for y in range(CY):
            n_send[k, :, LANES * y : LANES * (y + 1)] = spectrum[
                ZB * y : ZB * (y + 1), LANES * k : LANES * (k + 1)
            ]

    def exchange_narrow(source, target, phase):
        for d in range(1, narrow):
            to_n = lax.rem(n + d, narrow)
            remote(
                source.at[to_n], target.at[n], phase_send.at[phase], phase_recv.at[phase], w, to_n
            ).start()
        target[pl.ds(n, 1)] = source[pl.ds(n, 1)]
        pltpu.make_async_copy(
            target.at[pl.ds(0, narrow - 1)],
            target.at[pl.ds(0, narrow - 1)],
            phase_recv.at[phase],
        ).wait()

    exchange_narrow(n_send, n_recv, 1)
    locals_[2].wait()
    spanwise = exact_dot(
        zmat[:, 0:wide], n_recv[...].reshape(narrow * ZB, CY * LANES)
    )
    for y in range(CY):
        w_send[:, y] = spanwise[:, LANES * y : LANES * (y + 1)].reshape(wide, 1, LANES)

    def post_forward(d, carry):
        to_w = lax.rem(w + d, wide)
        remote(
            w_send.at[to_w], w_recv.at[w], phase_send.at[2], phase_recv.at[2], to_w, n
        ).start()
        return carry

    lax.fori_loop(1, wide, post_forward, 0)
    w_recv[pl.ds(w, 1)] = w_send[pl.ds(w, 1)]
    pltpu.make_async_copy(
        w_recv.at[pl.ds(0, wide - 1)], w_recv.at[pl.ds(0, wide - 1)], phase_recv.at[2]
    ).wait()

    rhs = w_recv[...].reshape(height, LANES)
    stride = 1
    level = 0
    while stride < height:
        rhs = (
            rhs
            + factors[level, 0] * shift_rows(rhs, stride, 0.0)
            + factors[level, 1] * shift_rows(rhs, -stride, 0.0)
        )
        stride *= 2
        level += 1
    phi = rhs * final[...]
    v_send[pl.ds(1, height)] = phi.reshape(height, 1, LANES)
    v_send[0] = phi[0:1]
    v_send[height + 1] = phi[height - 1 : height]

    def post_backward(d, carry):
        to_w = lax.rem(w + d, wide)
        remote(
            v_send.at[pl.ds(CY * to_w, CY + 2)],
            v_recv.at[w],
            phase_send.at[3],
            phase_recv.at[3],
            to_w,
            n,
        ).start()
        return carry

    lax.fori_loop(1, wide, post_backward, 0)
    v_recv[pl.ds(w, 1)] = v_send[pl.ds(CY * w, CY + 2)].reshape(1, CY + 2, 1, LANES)
    pltpu.make_async_copy(
        v_recv.at[pl.ds(0, wide - 1)], v_recv.at[pl.ds(0, wide - 1)], phase_recv.at[3]
    ).wait()

    planes = [v_recv[:, k].reshape(wide, LANES) for k in range(CY + 2)]
    cells = exact_dot(zmat[:, 128 : 128 + wide], jnp.concatenate(planes, 1))
    rims = exact_dot(
        zmat[:, 256 : 256 + CY * wide], jnp.concatenate(planes[1 : CY + 1], 0)
    )
    for k in range(narrow):
        u_send[k, :, 0 : (CY + 2) * LANES] = cells[ZB * k : ZB * (k + 1)]
        u_send[k, :, (CY + 2) * LANES :] = rims[ZB * k : ZB * (k + 1)]
    exchange_narrow(u_send, u_recv, 4)

    locals_[5].wait()
    locals_[6].wait()
    rows = [
        jnp.concatenate(
            [u_recv[k, :, LANES * r : LANES * (r + 1)] for k in range(narrow)], 1
        )
        for r in range(CY + 3)
    ]
    potential = split_dot(jnp.concatenate(rows, 0), ihigh, ilow)
    length_x = potential.shape[1]
    rim = potential[(CY + 2) * ZB :]
    row_id = lax.broadcasted_iota(jnp.int32, (ZB, length_x), 0)

    for y in range(CY):
        here = potential[(y + 1) * ZB : (y + 2) * ZB]
        below = potential[y * ZB : (y + 1) * ZB]
        above = potential[(y + 2) * ZB : (y + 3) * ZB]
        press_ref[y] = here
        left = jnp.where(row_id == 0, rim[2 * y : 2 * y + 1], pltpu.roll(here, 1, 0))
        right = jnp.where(
            row_id == ZB - 1, rim[2 * y + 1 : 2 * y + 2], pltpu.roll(here, ZB - 1, 0)
        )
        grads = [
            pltpu.roll(here, length_x - 1, 1) - pltpu.roll(here, 1, 1),
            above - below,
            right - left,
        ]
        for f in range(5):
            for s in range(SUBS):
                first = ((f * 5 + y + 1) * (ZB + 2) + 1) * SUBS + s
                value = pred[pl.ds(first, ZB, stride=SUBS), :]
                lanes = slice(LANES * s, LANES * (s + 1))
                if f < 3:
                    value = value - 0.5 * grads[f][:, lanes]
                out_ref[f, y, :, lanes] = value

    for halo in halos:
        halo.wait_send()
    part = sums.at[pl.ds(0, 3 * narrow - 1)]
    pltpu.make_async_copy(part, part, phase_send.at[0]).wait()
    for phase, ref in ((1, n_send), (4, u_send)):
        part = ref.at[pl.ds(0, narrow - 1)]
        pltpu.make_async_copy(part, part, phase_send.at[phase]).wait()
    for phase, ref in ((2, w_recv), (3, v_recv)):
        part = ref.at[pl.ds(0, wide - 1)]
        pltpu.make_async_copy(part, part, phase_send.at[phase]).wait()


def body(wide, narrow, consts, fields, y_bands):
    span_here, length_x = fields.shape[2], fields.shape[3]
    tiled = fields.reshape(5, CY, span_here, SUBS, LANES).transpose(0, 1, 3, 2, 4)
    tiled = tiled.reshape(5 * CY * SUBS * span_here, LANES)
    f32 = jnp.float32
    levels = math.ceil(math.log2(wide * CY))
    points = 5 * 5 * (ZB + 2) * SUBS
    vmem = pltpu.VMEM
    scratch = [
        vmem(tiled.shape, f32),
        *[vmem((length_x, length_x), jnp.bfloat16) for _ in range(4)],
        vmem(consts[4].shape, f32),
        vmem(consts[5].shape, f32),
        vmem((5, CY + 6, ZB + 6, SUBS, LANES), f32),
        vmem((3, CY + 2, ZB + 4, SUBS, LANES), f32),
        vmem((6, CY, ZB + 2, SUBS, LANES), f32),
        vmem((6, CY, ZB + 2, SUBS, LANES), f32),
        vmem((CY + 2, ZB + 2, SUBS, LANES), f32),
        vmem((3, CY + 2, ZB + 2, SUBS, LANES), f32),
        vmem((points, LANES), f32),
        vmem((points, LANES), f32),
        vmem((points, LANES), f32),
        vmem((CY * ZB * SUBS, LANES), f32),
        vmem((3 * narrow, SUBS, LANES), f32),
        vmem((SUBS, LANES), f32),
        vmem((levels, 2, wide * CY, LANES), f32),
        vmem((wide * CY, LANES), f32),
        vmem((narrow, ZB, CY * LANES), f32),
        vmem((narrow, ZB, CY * LANES), f32),
        vmem((wide, CY, 1, LANES), f32),
        vmem((wide, CY, 1, LANES), f32),
        vmem((wide * CY + 2, 1, LANES), f32),
        vmem((wide, CY + 2, 1, LANES), f32),
        vmem((narrow, ZB, (CY + 3) * LANES), f32),
        vmem((narrow, ZB, (CY + 3) * LANES), f32),
        pltpu.SemaphoreType.DMA((7,)),
        pltpu.SemaphoreType.DMA((16,)),
        pltpu.SemaphoreType.DMA((16,)),
        pltpu.SemaphoreType.DMA((5,)),
        pltpu.SemaphoreType.DMA((5,)),
    ]
    hbm = pl.BlockSpec(memory_space=pltpu.HBM)
    inside = pl.BlockSpec(memory_space=pltpu.VMEM)
    return pl.pallas_call(
        functools.partial(kernel, wide, narrow),
        out_shape=(
            jax.ShapeDtypeStruct(fields.shape, f32),
            jax.ShapeDtypeStruct(fields.shape[1:], f32),
        ),
        in_specs=[hbm, inside, *[hbm] * 6],
        out_specs=(inside, inside),
        scratch_shapes=scratch,
        compiler_params=pltpu.CompilerParams(
            collective_id=0, has_side_effects=True, vmem_limit_bytes=48 * 1024 * 1024
        ),
    )(tiled, y_bands, *consts)


def solution(mesh):
    wide, narrow = mesh.shape["wide"], mesh.shape["narrow"]

    def run(fields, y_bands):
        consts = tables(fields.shape[3], fields.shape[2], wide, narrow)
        consts = [jnp.asarray(table) for table in consts]
        return jax.shard_map(
            functools.partial(body, wide, narrow, consts),
            mesh=mesh,
            in_specs=(P(None, "wide", "narrow", None), P()),
            out_specs=(P(None, "wide", "narrow", None), P("wide", "narrow", None)),
            check_vma=False,
        )(fields, y_bands)

    return run
```

profile of v0, /device:TPU:1, one launch (start us, length us, event | category | flops | bytes accessed | tf_op | source)
XLA Modules:
  0.0 79.6 jit_solution(6687495026084626193)
XLA Ops:
  0.6 0.0 copy-start
  0.6 1.6 %copy-done = bf16[1024,1024]{1,0:T(8,128)(2,1)S(1)} copy-done((bf16[1024,1024]{1,0:T(8,128)(2,1)S(1)}, bf16[1024,1024]{1,0:T(8,128)(2,1)}, u32[]{:S(2)}) %copy-start) | copy-done | bytes 2097176
  2.2 0.0 copy-start.1
  2.2 1.6 %copy-done.1 = bf16[1024,1024]{1,0:T(8,128)(2,1)S(1)} copy-done((bf16[1024,1024]{1,0:T(8,128)(2,1)S(1)}, bf16[1024,1024]{1,0:T(8,128)(2,1)}, u32[]{:S(2)}) %copy-start.1) | copy-done | bytes 2097176
  3.8 0.0 copy-start.2
  3.8 1.0 %copy-done.2 = f32[5,3,8,1024]{3,2,1,0:T(8,128)S(1)} copy-done((f32[5,3,8,1024]{3,2,1,0:T(8,128)S(1)}, f32[5,3,8,1024]{3,2,1,0:T(8,128)}, u32[]{:S(2)}) %copy-start.2) | copy-done | bytes 491544
  4.8 0.0 copy-start.3
  4.8 0.9 %copy-done.3 = f32[64,512]{1,0:T(8,128)S(1)} copy-done((f32[64,512]{1,0:T(8,128)S(1)}, f32[64,512]{1,0:T(8,128)}, u32[]{:S(2)}) %copy-start.3) | copy-done | bytes 131096
  5.8 0.0 copy-start.4
  5.8 0.9 %copy-done.4 = f32[144,128]{1,0:T(8,128)S(1)} copy-done((f32[144,128]{1,0:T(8,128)S(1)}, f32[144,128]{1,0:T(8,128)}, u32[]{:S(2)}) %copy-start.4) | copy-done | bytes 73752
  6.6 0.0 copy-start.5
  6.6 0.7 copy-done.5
  7.3 70.8 %shard_map.95 = (f32[5,3,8,1024]{3,2,1,0:T(8,128)S(1)}, f32[3,8,1024]{2,1,0:T(8,128)S(1)}) custom-call(f32[960,128]{1,0:T(8,128)S(1)} %bitcast.5, f32[3,192]{1,0:T(4,128)S(1)} %copy-done.5, bf16[1024,1024]{1,0:T(8,128)(2,1)S(1)} %copy-done.1, bf16[1024,1024]{1,0:T(8,128)(2,1)S(1)} %copy-done, bf16[1024,1024]{1,0:T(8,128)(2,1)} %constant.14.clone.ihigh_hbm, ...), custom_call_target="tpu_custom_call" | custom-call | tf_op jit(solution)/shard_map/pallas_call | solution.py:690
  78.2 0.8 copy.12
  79.0 0.6 copy.13
Async XLA Ops:
  0.6 1.6 %copy-start = (bf16[1024,1024]{1,0:T(8,128)(2,1)S(1)}, bf16[1024,1024]{1,0:T(8,128)(2,1)}, u32[]{:S(2)}) copy-start(bf16[1024,1024]{1,0:T(8,128)(2,1)} %constant.13.clone.flow_hbm) | copy-start | bytes 6291460
  2.2 1.6 %copy-start.1 = (bf16[1024,1024]{1,0:T(8,128)(2,1)S(1)}, bf16[1024,1024]{1,0:T(8,128)(2,1)}, u32[]{:S(2)}) copy-start(bf16[1024,1024]{1,0:T(8,128)(2,1)} %constant.12.clone.fhigh_hbm) | copy-start | bytes 6291460
  3.8 1.0 %copy-start.2 = (f32[5,3,8,1024]{3,2,1,0:T(8,128)S(1)}, f32[5,3,8,1024]{3,2,1,0:T(8,128)}, u32[]{:S(2)}) copy-start(f32[5,3,8,1024]{3,2,1,0:T(8,128)} %param.8) | copy-start | bytes 1474564
  4.8 0.9 %copy-start.3 = (f32[64,512]{1,0:T(8,128)S(1)}, f32[64,512]{1,0:T(8,128)}, u32[]{:S(2)}) copy-start(f32[64,512]{1,0:T(8,128)} %constant.17.clone.zmat_hbm) | copy-start | bytes 393220
  5.8 0.9 %copy-start.4 = (f32[144,128]{1,0:T(8,128)S(1)}, f32[144,128]{1,0:T(8,128)}, u32[]{:S(2)}) copy-start(f32[144,128]{1,0:T(8,128)} %constant.16.clone.rows_hbm) | copy-start | bytes 221188
  6.6 0.7 copy-start.5
where the time goes:
time: 79.9 us; the launch traced here: 79.6 us
  Pallas kernels  70.8 us (89%)
  local copies, waits for them, and re-layouts  8.1 us (10%)
    pallas_call x1, Pallas kernels, body(): pl.pallas_call(functools.partial(kernel, wide, narrow), out_shape=(jax.Sh...  70.8 us
    unnamed x14, local copies, waits for them, and re-layouts  8.1 us

commit v1 on v0

--- a/solution.py
+++ b/solution.py
@@ -168,6 +168,7 @@
     u_send,
     u_recv,
     local_sem,
+    round_sem,
     halo_send,
     halo_recv,
     phase_send,
@@ -206,16 +207,26 @@
             device_id_type=pl.DeviceIdType.MESH,
         )
 
-    def greet_wide(d, carry):
-        greet(lax.rem(w + d, wide), n)
-        return carry
-
     for d in range(1, narrow):
         to_n = lax.rem(n + d, narrow)
         greet(w_down, to_n)
         greet(w_up, to_n)
         greet(w, to_n)
-    lax.fori_loop(1, wide, greet_wide, 0)
+    greet(w_up, n)
+    rounds = [1 << r for r in range(wide.bit_length() - 1)]
+    for reach in rounds:
+        greet(lax.rem(w + wide - reach, wide), n)
+
+    def tell(r):
+        pl.semaphore_signal(
+            round_sem.at[r],
+            inc=1,
+            device_id={"wide": lax.rem(w + rounds[r], wide), "narrow": n},
+            device_id_type=pl.DeviceIdType.MESH,
+        )
+
+    def hear(r):
+        pl.semaphore_wait(round_sem.at[r], 1)
 
     def remote(src, dst, send, recv, to_w, to_n):
         return pltpu.make_async_remote_copy(
@@ -236,8 +247,12 @@
         return carry
 
     lax.fori_loop(0, 5, to_tiles, 0)
-
-    pl.semaphore_wait(barrier, (wide - 1) + 3 * (narrow - 1))
+    for f in range(3):
+        for y in (1, 7):
+            for z in (1, 12):
+                pad[f, y, z] = jnp.zeros((SUBS, LANES), jnp.float32)
+
+    pl.semaphore_wait(barrier, 3 * (narrow - 1) + 1 + len(rounds))
 
     def both(fs, ys, zs):
         return pad.at[pl.ds(*fs), pl.ds(*ys), pl.ds(*zs)]
@@ -245,32 +260,44 @@
     own_z = (3, ZB)
     own_y = (3, CY)
     vel, sca = (0, 3), (3, 2)
-    plan = [
+    first = [
         (vel, (3, 2), own_z, (6, 2), own_z, w_down, n),
         (vel, (4, 2), own_z, (1, 2), own_z, w_up, n),
-        (vel, (3, 2), (3, 2), (6, 2), (11, 2), w_down, n_down),
-        (vel, (3, 2), (9, 2), (6, 2), (1, 2), w_down, n_up),
-        (vel, (4, 2), (3, 2), (1, 2), (11, 2), w_up, n_down),
-        (vel, (4, 2), (9, 2), (1, 2), (1, 2), w_up, n_up),
+        (vel, (3, 1), (3, 2), (6, 1), (11, 2), w_down, n_down),
+        (vel, (3, 1), (9, 2), (6, 1), (1, 2), w_down, n_up),
+        (vel, (5, 1), (3, 2), (2, 1), (11, 2), w_up, n_down),
+        (vel, (5, 1), (9, 2), (2, 1), (1, 2), w_up, n_up),
+        (vel, (4, 1), (3, 1), (7, 1), (11, 1), w_down, n_down),
+        (vel, (4, 1), (10, 1), (7, 1), (2, 1), w_down, n_up),
+        (vel, (4, 1), (3, 1), (1, 1), (11, 1), w_up, n_down),
+        (vel, (4, 1), (10, 1), (1, 1), (2, 1), w_up, n_up),
         (vel, own_y, (3, 2), own_y, (11, 2), w, n_down),
         (vel, own_y, (9, 2), own_y, (1, 2), w, n_up),
-        (sca, (3, 2), own_z, (6, 2), own_z, w_down, n),
-        (sca, (4, 2), own_z, (1, 2), own_z, w_up, n),
-        (sca, own_y, (3, 2), own_y, (11, 2), w, n_down),
-        (sca, own_y, (9, 2), own_y, (1, 2), w, n_up),
+    ]
+    second = [
         ((1, 1), (5, 1), own_z, (8, 1), own_z, w_down, n),
         ((1, 1), (3, 1), own_z, (0, 1), own_z, w_up, n),
+        ((3, 1), (3, 1), own_z, (6, 1), own_z, w_down, n),
+        ((3, 1), (5, 1), own_z, (2, 1), own_z, w_up, n),
         ((2, 1), own_y, (5, 1), own_y, (13, 1), w, n_down),
         ((2, 1), own_y, (8, 1), own_y, (0, 1), w, n_up),
     ]
-    halos = []
-    for k, (fs, sy, sz, ty, tz, to_w, to_n) in enumerate(plan):
-        halos.append(
-            remote(
-                both(fs, sy, sz), both(fs, ty, tz), halo_send.at[k], halo_recv.at[k], to_w, to_n
-            )
-        )
-        halos[-1].start()
+    third = [
+        ((3, 1), (4, 1), own_z, (7, 1), own_z, w_down, n),
+        ((3, 1), (4, 1), own_z, (1, 1), own_z, w_up, n),
+        ((4, 1), (3, 2), own_z, (6, 2), own_z, w_down, n),
+        ((4, 1), (4, 2), own_z, (1, 2), own_z, w_up, n),
+        (sca, own_y, (3, 2), own_y, (11, 2), w, n_down),
+        (sca, own_y, (9, 2), own_y, (1, 2), w, n_up),
+    ]
+    halos = [
+        remote(both(fs, sy, sz), both(fs, ty, tz), halo_send.at[k], halo_recv.at[k], to_w, to_n)
+        for k, (fs, sy, sz, ty, tz, to_w, to_n) in enumerate(first + second + third)
+    ]
+    cut_a, cut_b = len(first), len(first) + len(second)
+    for halo in halos[:cut_a]:
+        halo.start()
+    tell(0)
 
     locals_[1].wait()
     band = lax.broadcasted_iota(jnp.int32, (3, LANES), 0)
@@ -306,8 +333,18 @@
     weight = rowtab[pl.ds(narrow + n, 1), :] * rowtab[pl.ds(2 * narrow + wide + w, 1), :]
     final[...] = -weight / diag
 
-    for k in range(8):
-        halos[k].wait_recv()
+    hear(0)
+    tell(1)
+    for halo in halos[:cut_a]:
+        halo.wait_send()
+    for halo in halos[cut_a:]:
+        halo.start()
+    hear(1)
+    tell(2)
+    for halo in halos[:cut_a]:
+        halo.wait_recv()
+    hear(2)
+    tell(3)
 
     def clear(start, fields, first):
         def one(z, carry):
@@ -397,11 +434,17 @@
     tile = jnp.broadcast_to(jnp.sum(tile, 1, keepdims=True), (SUBS, LANES))
     mine[...] = tile
     sums[pl.ds(narrow + n, 1)] = tile[None]
-    peers = [(w_down, 2), (w, 1), (w_up, 0)]
-    for d in range(narrow):
-        to_n = lax.rem(n + d, narrow)
+    half_n = narrow // 2
+    side_n, cell_n = lax.div(n, half_n), lax.rem(n, half_n)
+    others = []
+    for d_side, d_cell in ((1, 2), (1, 1), (1, 3), (0, 2), (1, 0), (0, 1), (0, 3)):
+        others.append(
+            lax.rem(side_n + d_side, 2) * half_n + lax.rem(cell_n + d_cell, half_n)
+        )
+    peers = [(w_down, 2), (w_up, 0), (w, 1)]
+    for to_n in (*others, n):
         for to_w, slot in peers:
-            if d == 0 and slot == 1:
+            if to_n is n and slot == 1:
                 continue
             remote(
                 mine,
@@ -412,17 +455,19 @@
                 to_n,
             ).start()
 
-    for k in range(8, 16):
-        halos[k].wait_recv()
+    hear(3)
+    tell(4)
+    for halo in halos[cut_a:cut_b]:
+        halo.wait_recv()
 
     @pl.when(w == 0)
     def _():
-        clear(2, sca, 1)
+        clear(1, (3, 1), 2)
         clear(1, (1, 1), 0)
 
     @pl.when(w == wide - 1)
     def _():
-        clear(2, sca, 6)
+        clear(1, (3, 1), 6)
         clear(1, (1, 1), 8)
 
     def slot_of(f, y, z):
@@ -449,7 +494,7 @@
 
     def advance_cells(z, carry):
         for y in range(CY):
-            advance(range(5), y, z)
+            advance(range(3), y, z)
         advance((1,), -1, z)
         advance((1,), CY, z)
         return carry
@@ -459,6 +504,8 @@
         advance((2,), y, -1)
         advance((2,), y, ZB)
 
+    hear(4)
+    tell(5)
     pltpu.make_async_copy(
         sums.at[pl.ds(0, 3 * narrow - 1)], sums.at[pl.ds(0, 3 * narrow - 1)], phase_recv.at[0]
     ).wait()
@@ -480,7 +527,7 @@
 
     def finish_cells(z, carry):
         for y in range(CY):
-            for f in range(5):
+            for f in range(3):
                 finish(f, y, z)
         finish(1, -1, z, inside_low)
         finish(1, CY, z, inside_high)
@@ -519,8 +566,7 @@
             ]
 
     def exchange_narrow(source, target, phase):
-        for d in range(1, narrow):
-            to_n = lax.rem(n + d, narrow)
+        for to_n in others:
             remote(
                 source.at[to_n], target.at[n], phase_send.at[phase], phase_recv.at[phase], w, to_n
             ).start()
@@ -539,15 +585,59 @@
     for y in range(CY):
         w_send[:, y] = spanwise[:, LANES * y : LANES * (y + 1)].reshape(wide, 1, LANES)
 
-    def post_forward(d, carry):
-        to_w = lax.rem(w + d, wide)
+    depth = wide // 8
+    w_z, w_y, w_c = lax.div(w, 8), lax.rem(lax.div(w, 2), 4), lax.rem(w, 2)
+
+    def swing(k):
+        return lax.div(k, 2) * (1 - 2 * lax.rem(k, 2)) - lax.rem(k, 2)
+
+    def partner(k):
+        to_z = lax.rem(w_z + depth // 2 + swing(lax.div(k, 8)) + depth, depth)
+        to_y = lax.rem(w_y + 2 + swing(lax.rem(lax.div(k, 2), 4)) + 4, 4)
+        to_c = lax.rem(w_c + 1 - lax.rem(k, 2), 2)
+        return (to_z * 4 + to_y) * 2 + to_c
+
+    def post_forward(k, carry):
+        to_w = partner(k)
         remote(
             w_send.at[to_w], w_recv.at[w], phase_send.at[2], phase_recv.at[2], to_w, n
         ).start()
         return carry
 
-    lax.fori_loop(1, wide, post_forward, 0)
+    hear(5)
+    lax.fori_loop(0, wide - 1, post_forward, 0)
     w_recv[pl.ds(w, 1)] = w_send[pl.ds(w, 1)]
+
+    for halo in halos[cut_b:]:
+        halo.wait_recv()
+
+    @pl.when(w == 0)
+    def _():
+        clear(2, sca, 1)
+
+    @pl.when(w == wide - 1)
+    def _():
+        clear(2, sca, 6)
+
+    def scalar_cells(z, carry):
+        for y in range(CY):
+            advance((3, 4), y, z)
+            for f in (3, 4):
+                finish(f, y, z)
+        return carry
+
+    lax.fori_loop(0, ZB, scalar_cells, 0)
+
+    def to_rows(f, carry):
+        for y in range(CY):
+            for s in range(SUBS):
+                start = ((f * 5 + y + 1) * (ZB + 2) + 1) * SUBS + s
+                out_ref[f, y, :, LANES * s : LANES * (s + 1)] = pred[
+                    pl.ds(start, ZB, stride=SUBS), :
+                ]
+        return carry
+
+    lax.fori_loop(0, 5, to_rows, 0)
     pltpu.make_async_copy(
         w_recv.at[pl.ds(0, wide - 1)], w_recv.at[pl.ds(0, wide - 1)], phase_recv.at[2]
     ).wait()
@@ -568,8 +658,8 @@
     v_send[0] = phi[0:1]
     v_send[height + 1] = phi[height - 1 : height]
 
-    def post_backward(d, carry):
-        to_w = lax.rem(w + d, wide)
+    def post_backward(k, carry):
+        to_w = partner(k)
         remote(
             v_send.at[pl.ds(CY * to_w, CY + 2)],
             v_recv.at[w],
@@ -580,7 +670,7 @@
         ).start()
         return carry
 
-    lax.fori_loop(1, wide, post_backward, 0)
+    lax.fori_loop(0, wide - 1, post_backward, 0)
     v_recv[pl.ds(w, 1)] = v_send[pl.ds(CY * w, CY + 2)].reshape(1, CY + 2, 1, LANES)
     pltpu.make_async_copy(
         v_recv.at[pl.ds(0, wide - 1)], v_recv.at[pl.ds(0, wide - 1)], phase_recv.at[3]
@@ -623,16 +713,10 @@
             above - below,
             right - left,
         ]
-        for f in range(5):
-            for s in range(SUBS):
-                first = ((f * 5 + y + 1) * (ZB + 2) + 1) * SUBS + s
-                value = pred[pl.ds(first, ZB, stride=SUBS), :]
-                lanes = slice(LANES * s, LANES * (s + 1))
-                if f < 3:
-                    value = value - 0.5 * grads[f][:, lanes]
-                out_ref[f, y, :, lanes] = value
-
-    for halo in halos:
+        for f in range(3):
+            out_ref[f, y] = out_ref[f, y] - 0.5 * grads[f]
+
+    for halo in halos[cut_a:]:
         halo.wait_send()
     part = sums.at[pl.ds(0, 3 * narrow - 1)]
     pltpu.make_async_copy(part, part, phase_send.at[0]).wait()
@@ -680,8 +764,9 @@
         vmem((narrow, ZB, (CY + 3) * LANES), f32),
         vmem((narrow, ZB, (CY + 3) * LANES), f32),
         pltpu.SemaphoreType.DMA((7,)),
-        pltpu.SemaphoreType.DMA((16,)),
-        pltpu.SemaphoreType.DMA((16,)),
+        pltpu.SemaphoreType.REGULAR((wide.bit_length() - 1,)),
+        pltpu.SemaphoreType.DMA((24,)),
+        pltpu.SemaphoreType.DMA((24,)),
         pltpu.SemaphoreType.DMA((5,)),
         pltpu.SemaphoreType.DMA((5,)),
     ]
@@ -697,7 +782,7 @@
         out_specs=(inside, inside),
         scratch_shapes=scratch,
         compiler_params=pltpu.CompilerParams(
-            collective_id=0, has_side_effects=True, vmem_limit_bytes=48 * 1024 * 1024
+            collective_id=0, has_side_effects=True, vmem_limit_bytes=61 * 1024 * 1024
         ),
     )(tiled, y_bands, *consts)
 

time: 79.9 us -> 71.5 us (0.89)
  local copies, waits for them, and re-layouts: 8.1 us -> 3.39 us
  Pallas kernels: 70.8 us -> 67.2 us
    unnamed x14 -> x2, local copies, waits for them, and re-layouts: 8.1 us -> 3.39 us
    pallas_call x1, Pallas kernels: 70.8 us -> 67.2 us  [body(): pl.pallas_call(functools.partial(kernel, wide, narrow), out_shape=(jax.Sh...]
where the time goes in v1:
time: 71.5 us; the launch traced here: 71.2 us
  Pallas kernels  67.2 us (94%)
  local copies, waits for them, and re-layouts  3.39 us (5%)
    pallas_call x1, Pallas kernels, body(): pl.pallas_call(functools.partial(kernel, wide, narrow), out_shape=(jax.Sh...  67.2 us
    unnamed x2, local copies, waits for them, and re-layouts  3.39 us

profile of v1, /device:TPU:1, one launch (start us, length us, event | category | flops | bytes accessed | tf_op | source)
XLA Modules:
  0.0 71.2 jit_solution(590789405054587589)
XLA Ops:
  0.6 67.2 %shard_map.95 = (f32[5,3,8,1024]{3,2,1,0:T(8,128)}, f32[3,8,1024]{2,1,0:T(8,128)}) custom-call(f32[960,128]{1,0:T(8,128)} %bitcast.5, f32[3,192]{1,0:T(4,128)} %bands_ref.1, bf16[1024,1024]{1,0:T(8,128)(2,1)} %constant.12.clone.fhigh_hbm, bf16[1024,1024]{1,0:T(8,128)(2,1)} %constant.13.clone.flow_hbm, bf16[1024,1024]{1,0:T(8,128)(2,1)} %constant.14.clone.ihigh_hbm, ...), custom_call_target="tpu_custom_call" | custom-call | tf_op jit(solution)/shard_map/pallas_call | solution.py:775
  67.9 1.9 %copy.12 = f32[5,3,8,1024]{3,2,1,0:T(8,128)} copy(f32[5,3,8,1024]{3,2,1,0:T(8,128)} %get-tuple-element.4) | data formatting | bytes 983040
  69.7 1.5 %copy.13 = f32[3,8,1024]{2,1,0:T(8,128)} copy(f32[3,8,1024]{2,1,0:T(8,128)} %get-tuple-element.5) | data formatting | bytes 196608

commit v2 on v1

--- a/solution.py
+++ b/solution.py
@@ -60,7 +60,10 @@
                 z = (ZB * n - 1 if side == 0 else ZB * n + ZB) % span_all
                 row = ZB * n + 2 * y + side
                 zmat[row, 256 + y * span_all : 256 + (y + 1) * span_all] = basis_z[:, z]
-    return (*forward, *inverse, rows, zmat)
+    small = np.zeros((length_x, length_x), np.float32)
+    small[0 : rows.shape[0], 0:LANES] = rows
+    small[0:span_all, LANES : LANES + 512] = zmat
+    return (*forward, *inverse, small)
 
 
 def shift_x(value, step):
@@ -134,8 +137,7 @@
     flow_hbm,
     ihigh_hbm,
     ilow_hbm,
-    rows_hbm,
-    zmat_hbm,
+    small_hbm,
     out_ref,
     press_ref,
     nat,
@@ -157,8 +159,10 @@
     div,
     sums,
     mine,
+    bands,
+    block,
+    chain,
     factors,
-    final,
     n_send,
     n_recv,
     w_send,
@@ -176,7 +180,6 @@
 ):
     w = lax.axis_index("wide")
     n = lax.axis_index("narrow")
-    height = wide * CY
     w_down, w_up = lax.rem(w + wide - 1, wide), lax.rem(w + 1, wide)
     n_down, n_up = lax.rem(n + narrow - 1, narrow), lax.rem(n + 1, narrow)
 
@@ -185,8 +188,8 @@
         for k, (src, dst) in enumerate(
             [
                 (fields_hbm, nat),
-                (rows_hbm, rowtab),
-                (zmat_hbm, zmat),
+                (small_hbm.at[pl.ds(0, rowtab.shape[0]), pl.ds(0, LANES)], rowtab),
+                (small_hbm.at[pl.ds(0, zmat.shape[0]), pl.ds(LANES, 512)], zmat),
                 (fhigh_hbm, fhigh),
                 (flow_hbm, flow),
                 (ihigh_hbm, ihigh),
@@ -311,27 +314,51 @@
         )
         for k in range(3)
     ]
-    eig = rowtab[pl.ds(n, 1), :] + rowtab[pl.ds(2 * narrow + w, 1), :]
-    lower, diag, upper = spread[0], spread[1] + eig, spread[2]
+    for k in range(3):
+        bands[k] = spread[k]
+
+    def invert(low, mid, high):
+        det = 1.0 / (mid[0] * mid[1] - high[0] * low[1])
+        return mid[1] * det, -high[0] * det, -low[1] * det, mid[0] * det
+
+    lam_x = rowtab[pl.ds(n, 1), :]
+    eig = rowtab[2 * narrow : 2 * narrow + wide, :] + lam_x
+    own_low, own_mid, own_high = (
+        [bands[k, pl.ds(CY * w + j, 1), :] for j in range(CY)] for k in range(3)
+    )
+    for k, part in enumerate(invert(own_low, [m + eig for m in own_mid[:2]], own_high)):
+        block[k] = part
+    block[4] = -rowtab[2 * narrow + wide :, :] * rowtab[pl.ds(narrow + n, 1), :]
+
+    eig = lam_x + rowtab[pl.ds(2 * narrow + w, 1), :]
+    low, mid, high = (
+        [bands[k, pl.ds(j, wide, stride=CY), :] for j in range(CY)] for k in range(3)
+    )
+    mid = [m + eig for m in mid]
+    i00, i01, i10, i11 = invert(low, mid, high)
+    from_low, from_high = -i00 * low[0], -i01 * high[1]
+    chain[0], chain[1], chain[2] = from_low, from_high, -high[2]
+    lower = -low[2] * i10 * low[0]
+    diag = mid[2] - low[2] * i11 * high[1] + high[2] * shift_rows(from_low, -1, 0.0)
+    upper = high[2] * shift_rows(from_high, -1, 0.0)
     stride = 1
     level = 0
-    while stride < height:
+    while stride < wide:
         inv = 1.0 / diag
-        low = -lower * shift_rows(inv, stride, 1.0)
-        high = -upper * shift_rows(inv, -stride, 1.0)
-        factors[level, 0] = low
-        factors[level, 1] = high
+        to_low = -lower * shift_rows(inv, stride, 1.0)
+        to_high = -upper * shift_rows(inv, -stride, 1.0)
+        factors[level, 0] = to_low
+        factors[level, 1] = to_high
         diag = (
             diag
-            + low * shift_rows(upper, stride, 0.0)
-            + high * shift_rows(lower, -stride, 0.0)
-        )
-        lower = low * shift_rows(lower, stride, 0.0)
-        upper = high * shift_rows(upper, -stride, 0.0)
+            + to_low * shift_rows(upper, stride, 0.0)
+            + to_high * shift_rows(lower, -stride, 0.0)
+        )
+        lower = to_low * shift_rows(lower, stride, 0.0)
+        upper = to_high * shift_rows(upper, -stride, 0.0)
         stride *= 2
         level += 1
-    weight = rowtab[pl.ds(narrow + n, 1), :] * rowtab[pl.ds(2 * narrow + wide + w, 1), :]
-    final[...] = -weight / diag
+    chain[3] = 1.0 / diag
 
     hear(0)
     tell(1)
@@ -339,29 +366,26 @@
         halo.wait_send()
     for halo in halos[cut_a:]:
         halo.start()
-    hear(1)
-    tell(2)
-    for halo in halos[:cut_a]:
-        halo.wait_recv()
-    hear(2)
-    tell(3)
-
-    def clear(start, fields, first):
+
+    def clear(rows, fields, cells):
         def one(z, carry):
-            for f in range(fields[0], fields[0] + fields[1]):
-                for y in range(first, first + start):
+            for f in fields:
+                for y in rows:
                     pad[f, y, z] = jnp.zeros((SUBS, LANES), jnp.float32)
             return carry
 
-        lax.fori_loop(0, ZB + 6, one, 0)
-
-    @pl.when(w == 0)
-    def _():
-        clear(2, vel, 1)
-
-    @pl.when(w == wide - 1)
-    def _():
-        clear(2, vel, 6)
+        lax.fori_loop(cells[0], cells[1], one, 0)
+
+    def outside(below, above, fields, cells):
+        @pl.when(w == 0)
+        def _():
+            for part in cells:
+                clear(below, fields, part)
+
+        @pl.when(w == wide - 1)
+        def _():
+            for part in cells:
+                clear(above, fields, part)
 
     def at_pad(f, y, z):
         return pad[f, y + 3, z + 3]
@@ -374,7 +398,6 @@
                 yfilt[i, y, iz] = three(column[y], column[y + 1], column[y + 2])
         return carry
 
-    lax.fori_loop(0, ZB + 4, filter_rows, 0)
 
     def local_terms(iz, carry):
         z = iz - 1
@@ -397,7 +420,6 @@
                 filt[i, y, iz] = filter_x(value)
         return carry
 
-    lax.fori_loop(0, ZB + 2, local_terms, 0)
 
     def at_filt(f, y, z):
         return filt[f, y + 1, z + 1]
@@ -425,9 +447,26 @@
         return tuple(cross), tuple(square)
 
     nothing = jnp.zeros((SUBS, LANES), jnp.float32)
-    cross, square = lax.fori_loop(
-        0, ZB, plane_terms, ((nothing,) * CY, (nothing,) * CY)
-    )
+    plane = ((nothing,) * CY, (nothing,) * CY)
+
+    def edges(step, inner):
+        return lambda k, carry: step(k + lax.div(k, 2) * inner, carry)
+
+    inner_cells, rim_cells = (3, ZB + 3), ((1, 3), (ZB + 3, ZB + 5))
+    for halo in halos[:2]:
+        halo.wait_recv()
+    hear(1)
+    tell(2)
+    outside((1, 2), (6, 7), range(3), (inner_cells,))
+    lax.fori_loop(2, ZB + 2, filter_rows, 0)
+    lax.fori_loop(2, ZB, local_terms, 0)
+    plane = lax.fori_loop(2, ZB - 2, plane_terms, plane)
+    for halo in halos[2:cut_a]:
+        halo.wait_recv()
+    outside((1, 2), (6, 7), range(3), rim_cells)
+    lax.fori_loop(0, 4, edges(filter_rows, ZB), 0)
+    lax.fori_loop(0, 4, edges(local_terms, ZB - 2), 0)
+    cross, square = lax.fori_loop(0, 4, edges(plane_terms, ZB - 4), plane)
     packed = [jnp.sum(v, 0, keepdims=True) for v in (*cross, *square)]
     packed.append(jnp.zeros((SUBS - 2 * CY, LANES), jnp.float32))
     tile = jnp.concatenate(packed, 0)
@@ -455,20 +494,12 @@
                 to_n,
             ).start()
 
-    hear(3)
-    tell(4)
+    hear(2)
+    tell(3)
     for halo in halos[cut_a:cut_b]:
         halo.wait_recv()
-
-    @pl.when(w == 0)
-    def _():
-        clear(1, (3, 1), 2)
-        clear(1, (1, 1), 0)
-
-    @pl.when(w == wide - 1)
-    def _():
-        clear(1, (3, 1), 6)
-        clear(1, (1, 1), 8)
+    outside((2,), (6,), (3,), (inner_cells,))
+    outside((0,), (8,), (1,), (inner_cells,))
 
     def slot_of(f, y, z):
         return pl.ds(pl.multiple_of(((f * 5 + y + 1) * (ZB + 2) + z + 1) * SUBS, SUBS), SUBS)
@@ -504,8 +535,8 @@
         advance((2,), y, -1)
         advance((2,), y, ZB)
 
-    hear(4)
-    tell(5)
+    hear(3)
+    tell(4)
     pltpu.make_async_copy(
         sums.at[pl.ds(0, 3 * narrow - 1)], sums.at[pl.ds(0, 3 * narrow - 1)], phase_recv.at[0]
     ).wait()
@@ -577,13 +608,18 @@
             phase_recv.at[phase],
         ).wait()
 
+    hear(4)
+    tell(5)
     exchange_narrow(n_send, n_recv, 1)
     locals_[2].wait()
     spanwise = exact_dot(
         zmat[:, 0:wide], n_recv[...].reshape(narrow * ZB, CY * LANES)
     )
-    for y in range(CY):
-        w_send[:, y] = spanwise[:, LANES * y : LANES * (y + 1)].reshape(wide, 1, LANES)
+    rhs = [spanwise[:, LANES * y : LANES * (y + 1)] * block[4] for y in range(CY)]
+    inner_0 = block[0] * rhs[0] + block[1] * rhs[1]
+    inner_1 = block[2] * rhs[0] + block[3] * rhs[1]
+    w_send[:, 0] = inner_0.reshape(wide, 1, LANES)
+    w_send[:, 1] = (rhs[2] - own_low[2] * inner_1).reshape(wide, 1, LANES)
 
     depth = wide // 8
     w_z, w_y, w_c = lax.div(w, 8), lax.rem(lax.div(w, 2), 4), lax.rem(w, 2)
@@ -611,13 +647,7 @@
     for halo in halos[cut_b:]:
         halo.wait_recv()
 
-    @pl.when(w == 0)
-    def _():
-        clear(2, sca, 1)
-
-    @pl.when(w == wide - 1)
-    def _():
-        clear(2, sca, 6)
+    outside((1, 2), (6, 7), (3, 4), (inner_cells,))
 
     def scalar_cells(z, carry):
         for y in range(CY):
@@ -642,26 +672,30 @@
         w_recv.at[pl.ds(0, wide - 1)], w_recv.at[pl.ds(0, wide - 1)], phase_recv.at[2]
     ).wait()
 
-    rhs = w_recv[...].reshape(height, LANES)
+    first_row = w_recv[:, 0].reshape(wide, LANES)
+    last = w_recv[:, 1].reshape(wide, LANES) + chain[2] * shift_rows(first_row, -1, 0.0)
     stride = 1
     level = 0
-    while stride < height:
-        rhs = (
-            rhs
-            + factors[level, 0] * shift_rows(rhs, stride, 0.0)
-            + factors[level, 1] * shift_rows(rhs, -stride, 0.0)
+    while stride < wide:
+        last = (
+            last
+            + factors[level, 0] * shift_rows(last, stride, 0.0)
+            + factors[level, 1] * shift_rows(last, -stride, 0.0)
         )
         stride *= 2
         level += 1
-    phi = rhs * final[...]
-    v_send[pl.ds(1, height)] = phi.reshape(height, 1, LANES)
-    v_send[0] = phi[0:1]
-    v_send[height + 1] = phi[height - 1 : height]
+    last = last * chain[3]
+    before = shift_rows(last, 1, 0.0)
+    first_row = first_row + chain[0] * before + chain[1] * last
+    before = jnp.concatenate([first_row[0:1], last[: wide - 1]], 0)
+    after = jnp.concatenate([first_row[1:], last[wide - 1 :]], 0)
+    for k, part in enumerate((before, last, after)):
+        v_send[:, k] = part.reshape(wide, 1, LANES)
 
     def post_backward(k, carry):
         to_w = partner(k)
         remote(
-            v_send.at[pl.ds(CY * to_w, CY + 2)],
+            v_send.at[to_w],
             v_recv.at[w],
             phase_send.at[3],
             phase_recv.at[3],
@@ -671,12 +705,21 @@
         return carry
 
     lax.fori_loop(0, wide - 1, post_backward, 0)
-    v_recv[pl.ds(w, 1)] = v_send[pl.ds(CY * w, CY + 2)].reshape(1, CY + 2, 1, LANES)
+    v_recv[pl.ds(w, 1)] = v_send[pl.ds(w, 1)]
     pltpu.make_async_copy(
         v_recv.at[pl.ds(0, wide - 1)], v_recv.at[pl.ds(0, wide - 1)], phase_recv.at[3]
     ).wait()
 
-    planes = [v_recv[:, k].reshape(wide, LANES) for k in range(CY + 2)]
+    before, last, after = (v_recv[:, k].reshape(wide, LANES) for k in range(3))
+    rest_0 = rhs[0] - own_low[0] * before
+    rest_1 = rhs[1] - own_high[1] * last
+    planes = [
+        before,
+        block[0] * rest_0 + block[1] * rest_1,
+        block[2] * rest_0 + block[3] * rest_1,
+        last,
+        after,
+    ]
     cells = exact_dot(zmat[:, 128 : 128 + wide], jnp.concatenate(planes, 1))
     rims = exact_dot(
         zmat[:, 256 : 256 + CY * wide], jnp.concatenate(planes[1 : CY + 1], 0)
@@ -733,14 +776,14 @@
     tiled = fields.reshape(5, CY, span_here, SUBS, LANES).transpose(0, 1, 3, 2, 4)
     tiled = tiled.reshape(5 * CY * SUBS * span_here, LANES)
     f32 = jnp.float32
-    levels = math.ceil(math.log2(wide * CY))
+    levels = math.ceil(math.log2(wide))
     points = 5 * 5 * (ZB + 2) * SUBS
     vmem = pltpu.VMEM
     scratch = [
         vmem(tiled.shape, f32),
         *[vmem((length_x, length_x), jnp.bfloat16) for _ in range(4)],
-        vmem(consts[4].shape, f32),
-        vmem(consts[5].shape, f32),
+        vmem((2 * narrow + 2 * wide, LANES), f32),
+        vmem((wide, 512), f32),
         vmem((5, CY + 6, ZB + 6, SUBS, LANES), f32),
         vmem((3, CY + 2, ZB + 4, SUBS, LANES), f32),
         vmem((6, CY, ZB + 2, SUBS, LANES), f32),
@@ -753,14 +796,16 @@
         vmem((CY * ZB * SUBS, LANES), f32),
         vmem((3 * narrow, SUBS, LANES), f32),
         vmem((SUBS, LANES), f32),
-        vmem((levels, 2, wide * CY, LANES), f32),
-        vmem((wide * CY, LANES), f32),
+        vmem((3, wide * CY, LANES), f32),
+        vmem((5, wide, LANES), f32),
+        vmem((4, wide, LANES), f32),
+        vmem((levels, 2, wide, LANES), f32),
         vmem((narrow, ZB, CY * LANES), f32),
         vmem((narrow, ZB, CY * LANES), f32),
-        vmem((wide, CY, 1, LANES), f32),
-        vmem((wide, CY, 1, LANES), f32),
-        vmem((wide * CY + 2, 1, LANES), f32),
-        vmem((wide, CY + 2, 1, LANES), f32),
+        vmem((wide, 2, 1, LANES), f32),
+        vmem((wide, 2, 1, LANES), f32),
+        vmem((wide, 3, 1, LANES), f32),
+        vmem((wide, 3, 1, LANES), f32),
         vmem((narrow, ZB, (CY + 3) * LANES), f32),
         vmem((narrow, ZB, (CY + 3) * LANES), f32),
         pltpu.SemaphoreType.DMA((7,)),
@@ -778,11 +823,11 @@
             jax.ShapeDtypeStruct(fields.shape, f32),
             jax.ShapeDtypeStruct(fields.shape[1:], f32),
         ),
-        in_specs=[hbm, inside, *[hbm] * 6],
+        in_specs=[hbm, inside, *[hbm] * 5],
         out_specs=(inside, inside),
         scratch_shapes=scratch,
         compiler_params=pltpu.CompilerParams(
-            collective_id=0, has_side_effects=True, vmem_limit_bytes=61 * 1024 * 1024
+            collective_id=0, has_side_effects=True, vmem_limit_bytes=53 * 1024 * 1024
         ),
     )(tiled, y_bands, *consts)
 

time: 71.5 us -> 66.2 us (0.926)
  Pallas kernels: 67.2 us -> 63.3 us
  local copies, waits for them, and re-layouts: 3.39 us -> 2.1 us
    pallas_call x1, Pallas kernels: 67.2 us -> 63.3 us  [body(): pl.pallas_call(functools.partial(kernel, wide, narrow), out_shape=(jax.Sh...]
    unnamed x2 -> x4, local copies, waits for them, and re-layouts: 3.39 us -> 2.1 us
where the time goes in v2:
time: 66.2 us; the launch traced here: 66 us
  Pallas kernels  63.3 us (96%)
  local copies, waits for them, and re-layouts  2.1 us (3%)
    pallas_call x1, Pallas kernels, body(): pl.pallas_call(functools.partial(kernel, wide, narrow), out_shape=(jax.Sh...  63.3 us
    unnamed x4, local copies, waits for them, and re-layouts  2.1 us

profile of v2, /device:TPU:1, one launch (start us, length us, event | category | flops | bytes accessed | tf_op | source)
XLA Modules:
  0.0 66.0 jit_solution(10834041162816846986)
XLA Ops:
  0.6 0.0 copy-start
  0.6 0.7 %copy-done = f32[3,192]{1,0:T(4,128)S(1)} copy-done((f32[3,192]{1,0:T(4,128)S(1)}, f32[3,192]{1,0:T(4,128)}, u32[]{:S(2)}) %copy-start) | copy-done | bytes 2328
  1.3 63.3 %shard_map.86 = (f32[5,3,8,1024]{3,2,1,0:T(8,128)S(1)}, f32[3,8,1024]{2,1,0:T(8,128)S(1)}) custom-call(f32[960,128]{1,0:T(8,128)} %bitcast.5, f32[3,192]{1,0:T(4,128)S(1)} %copy-done, bf16[1024,1024]{1,0:T(8,128)(2,1)} %constant.10.clone.fhigh_hbm, bf16[1024,1024]{1,0:T(8,128)(2,1)} %constant.11.clone.flow_hbm, bf16[1024,1024]{1,0:T(8,128)(2,1)} %constant.12.clone.ihigh_hbm, ...), custom_call_target="tpu_custom_call" | custom-call | tf_op jit(solution)/shard_map/pallas_call | solution.py:820
  64.6 0.8 %copy.11 = f32[5,3,8,1024]{3,2,1,0:T(8,128)} copy(f32[5,3,8,1024]{3,2,1,0:T(8,128)S(1)} %get-tuple-element.4) | data formatting | bytes 983040
  65.4 0.6 copy.12
Async XLA Ops:
  0.6 0.7 %copy-start = (f32[3,192]{1,0:T(4,128)S(1)}, f32[3,192]{1,0:T(4,128)}, u32[]{:S(2)}) copy-start(f32[3,192]{1,0:T(4,128)} %bands_ref.1) | copy-start | bytes 6916

commit v3 on v2

--- a/solution.py
+++ b/solution.py
@@ -211,10 +211,10 @@
         )
 
     for d in range(1, narrow):
-        to_n = lax.rem(n + d, narrow)
+        greet(w, lax.rem(n + d, narrow))
+    for to_n in (n_down, n_up):
         greet(w_down, to_n)
         greet(w_up, to_n)
-        greet(w, to_n)
     greet(w_up, n)
     rounds = [1 << r for r in range(wide.bit_length() - 1)]
     for reach in rounds:
@@ -255,7 +255,7 @@
             for z in (1, 12):
                 pad[f, y, z] = jnp.zeros((SUBS, LANES), jnp.float32)
 
-    pl.semaphore_wait(barrier, 3 * (narrow - 1) + 1 + len(rounds))
+    pl.semaphore_wait(barrier, (narrow - 1) + 5 + len(rounds))
 
     def both(fs, ys, zs):
         return pad.at[pl.ds(*fs), pl.ds(*ys), pl.ds(*zs)]
@@ -364,7 +364,7 @@
     tell(1)
     for halo in halos[:cut_a]:
         halo.wait_send()
-    for halo in halos[cut_a:]:
+    for halo in halos[cut_a:cut_b]:
         halo.start()
 
     def clear(rows, fields, cells):
@@ -494,6 +494,8 @@
                 to_n,
             ).start()
 
+    for halo in halos[cut_b:]:
+        halo.start()
     hear(2)
     tell(3)
     for halo in halos[cut_a:cut_b]:
@@ -535,8 +537,42 @@
         advance((2,), y, -1)
         advance((2,), y, ZB)
 
+    inside_low = jnp.where(w == 0, 0.0, 1.0)
+    inside_high = jnp.where(w == wide - 1, 0.0, 1.0)
+
+    def store(row, value):
+        div[pl.ds(pl.multiple_of(row * SUBS, SUBS), SUBS), :] = value
+
+    def divergence(z, carry):
+        def get(part, f, y):
+            value = part[slot_of(f, y, z), :]
+            if y < 0:
+                return value * inside_low
+            return value * inside_high if y == CY else value
+
+        wall_a = [get(part_a, 1, y) for y in range(-1, CY + 1)]
+        for y in range(CY):
+            for first_row, part in ((0, part_a), (CY * ZB, part_b)):
+                stream = part[slot_of(0, y, z), :]
+                value = shift_x(stream, 1) - shift_x(stream, -1)
+                value = value + (part[slot_of(2, y, z + 1), :] - part[slot_of(2, y, z - 1), :])
+                if first_row == 0:
+                    value = value + (wall_a[y + 2] - wall_a[y])
+                store(first_row + y * ZB + z, 0.5 * value)
+        for y in range(-1, CY + 1):
+            store((2 * CY + y + 1) * ZB + z, 0.5 * get(part_b, 1, y))
+        return carry
+
+    lax.fori_loop(0, ZB, divergence, 0)
+    count = (3 * CY + 2) * ZB
     hear(3)
     tell(4)
+    locals_[3].wait()
+    locals_[4].wait()
+    flat = jnp.concatenate([div[pl.ds(s, count, stride=SUBS), :] for s in range(SUBS)], 1)
+    flat = jnp.concatenate([flat, jnp.zeros((8, flat.shape[1]), jnp.float32)], 0)
+    spectrum = split_dot(flat, fhigh, flow)
+
     pltpu.make_async_copy(
         sums.at[pl.ds(0, 3 * narrow - 1)], sums.at[pl.ds(0, 3 * narrow - 1)], phase_recv.at[0]
     ).wait()
@@ -549,52 +585,14 @@
             ratio = total[row : row + 1] / (total[CY + row : CY + row + 1] + EPSILON)
             coef.append(jnp.broadcast_to(ratio, (SUBS, LANES)))
 
-    def finish(f, y, z, scale=None):
-        value = part_a[slot_of(f, y, z), :] + coef[y + 1] * part_b[slot_of(f, y, z), :]
-        pred[slot_of(f, y, z), :] = value if scale is None else value * scale
-
-    inside_low = jnp.where(w == 0, 0.0, 1.0)
-    inside_high = jnp.where(w == wide - 1, 0.0, 1.0)
-
-    def finish_cells(z, carry):
+    for k in range(narrow):
+        part = spectrum[:, LANES * k : LANES * (k + 1)]
+        tiles = [part[ZB * r : ZB * (r + 1)] for r in range(3 * CY + 2)]
+        walls = [coef[r] * tiles[2 * CY + r] for r in range(CY + 2)]
         for y in range(CY):
-            for f in range(3):
-                finish(f, y, z)
-        finish(1, -1, z, inside_low)
-        finish(1, CY, z, inside_high)
-        return carry
-
-    lax.fori_loop(0, ZB, finish_cells, 0)
-    for y in range(CY):
-        finish(2, y, -1)
-        finish(2, y, ZB)
-
-    def at_pred(f, y, z):
-        return pred[slot_of(f, y, z), :]
-
-    def divergence(z, carry):
-        for y in range(CY):
-            stream = at_pred(0, y, z)
-            value = shift_x(stream, 1) - shift_x(stream, -1)
-            value = value + (at_pred(1, y + 1, z) - at_pred(1, y - 1, z))
-            value = value + (at_pred(2, y, z + 1) - at_pred(2, y, z - 1))
-            div[pl.ds(pl.multiple_of((y * ZB + z) * SUBS, SUBS), SUBS), :] = 0.5 * value
-        return carry
-
-    lax.fori_loop(0, ZB, divergence, 0)
-
-    locals_[3].wait()
-    locals_[4].wait()
-    flat = jnp.concatenate(
-        [div[pl.ds(s, CY * ZB, stride=SUBS), :] for s in range(SUBS)], 1
-    )
-    flat = jnp.concatenate([flat, jnp.zeros((8, flat.shape[1]), jnp.float32)], 0)
-    spectrum = split_dot(flat, fhigh, flow)
-    for k in range(narrow):
-        for y in range(CY):
-            n_send[k, :, LANES * y : LANES * (y + 1)] = spectrum[
-                ZB * y : ZB * (y + 1), LANES * k : LANES * (k + 1)
-            ]
+            n_send[k, :, LANES * y : LANES * (y + 1)] = (
+                tiles[y] + coef[y + 1] * tiles[CY + y] + (walls[y + 2] - walls[y])
+            )
 
     def exchange_narrow(source, target, phase):
         for to_n in others:
@@ -649,10 +647,15 @@
 
     outside((1, 2), (6, 7), (3, 4), (inner_cells,))
 
+    def finish(f, y, z):
+        pred[slot_of(f, y, z), :] = (
+            part_a[slot_of(f, y, z), :] + coef[y + 1] * part_b[slot_of(f, y, z), :]
+        )
+
     def scalar_cells(z, carry):
         for y in range(CY):
             advance((3, 4), y, z)
-            for f in (3, 4):
+            for f in range(5):
                 finish(f, y, z)
         return carry
 
@@ -793,7 +796,7 @@
         vmem((points, LANES), f32),
         vmem((points, LANES), f32),
         vmem((points, LANES), f32),
-        vmem((CY * ZB * SUBS, LANES), f32),
+        vmem(((3 * CY + 2) * ZB * SUBS, LANES), f32),
         vmem((3 * narrow, SUBS, LANES), f32),
         vmem((SUBS, LANES), f32),
         vmem((3, wide * CY, LANES), f32),

time: 66.2 us -> 62 us (0.937)
  Pallas kernels: 63.3 us -> 59.1 us
    pallas_call x1, Pallas kernels: 63.3 us -> 59.1 us  [body(): pl.pallas_call(functools.partial(kernel, wide, narrow), out_shape=(jax.Sh...]
where the time goes in v3:
time: 62 us; the launch traced here: 61.9 us
  Pallas kernels  59.1 us (95%)
  local copies, waits for them, and re-layouts  2.1 us (3%)
  between operations  0.65 us (1%)
    pallas_call x1, Pallas kernels, body(): pl.pallas_call(functools.partial(kernel, wide, narrow), out_shape=(jax.Sh...  59.1 us
    unnamed x4, local copies, waits for them, and re-layouts  2.1 us

profile of v3, /device:TPU:1, one launch (start us, length us, event | category | flops | bytes accessed | tf_op | source)
XLA Modules:
  0.0 61.9 jit_solution(18387831986928570829)
XLA Ops:
  0.6 0.0 copy-start
  0.6 0.7 %copy-done = f32[3,192]{1,0:T(4,128)S(1)} copy-done((f32[3,192]{1,0:T(4,128)S(1)}, f32[3,192]{1,0:T(4,128)}, u32[]{:S(2)}) %copy-start) | copy-done | bytes 2328
  1.3 59.1 %shard_map.86 = (f32[5,3,8,1024]{3,2,1,0:T(8,128)S(1)}, f32[3,8,1024]{2,1,0:T(8,128)S(1)}) custom-call(f32[960,128]{1,0:T(8,128)} %bitcast.5, f32[3,192]{1,0:T(4,128)S(1)} %copy-done, bf16[1024,1024]{1,0:T(8,128)(2,1)} %constant.10.clone.fhigh_hbm, bf16[1024,1024]{1,0:T(8,128)(2,1)} %constant.11.clone.flow_hbm, bf16[1024,1024]{1,0:T(8,128)(2,1)} %constant.12.clone.ihigh_hbm, ...), custom_call_target="tpu_custom_call" | custom-call | tf_op jit(solution)/shard_map/pallas_call | solution.py:823
  60.5 0.8 %copy.11 = f32[5,3,8,1024]{3,2,1,0:T(8,128)} copy(f32[5,3,8,1024]{3,2,1,0:T(8,128)S(1)} %get-tuple-element.4) | data formatting | bytes 983040
  61.2 0.6 %copy.12 = f32[3,8,1024]{2,1,0:T(8,128)} copy(f32[3,8,1024]{2,1,0:T(8,128)S(1)} %get-tuple-element.5) | data formatting | bytes 196608
Async XLA Ops:
  0.6 0.7 %copy-start = (f32[3,192]{1,0:T(4,128)S(1)}, f32[3,192]{1,0:T(4,128)}, u32[]{:S(2)}) copy-start(f32[3,192]{1,0:T(4,128)} %bands_ref.1) | copy-start | bytes 6916

commit v4 on v3

--- a/solution.py
+++ b/solution.py
@@ -111,10 +111,22 @@
     return jnp.concatenate([value[-step:], pad], 0)
 
 
+def halves(value):
+    high = value.astype(jnp.bfloat16)
+    return high, (value - high.astype(jnp.float32)).astype(jnp.bfloat16)
+
+
 def exact_dot(left, right):
-    return jnp.dot(
-        left, right, precision=lax.Precision.HIGHEST, preferred_element_type=jnp.float32
+    count = left.shape[0]
+    left_high, left_low = halves(left)
+    right_high, right_low = halves(right)
+    both = jnp.dot(
+        jnp.concatenate([left_high, left_low], 0),
+        right_high,
+        preferred_element_type=jnp.float32,
     )
+    rest = jnp.dot(left_high, right_low, preferred_element_type=jnp.float32)
+    return both[:count] + (both[count:] + rest)
 
 
 def split_dot(rows, high_ref, low_ref):
@@ -197,8 +209,7 @@
             ]
         )
     ]
-    for copy in locals_:
-        copy.start()
+    locals_[0].start()
 
     barrier = pltpu.get_barrier_semaphore()
 
@@ -301,6 +312,8 @@
     for halo in halos[:cut_a]:
         halo.start()
     tell(0)
+    for copy in locals_[1:]:
+        copy.start()
 
     locals_[1].wait()
     band = lax.broadcasted_iota(jnp.int32, (3, LANES), 0)

time: 62 us -> 61.9 us (level)
  no operation moved by 1% of the time
where the time goes in v4:
time: 61.9 us; the launch traced here: 61.7 us
  Pallas kernels  59 us (95%)
  local copies, waits for them, and re-layouts  2.1 us (3%)
  between operations  0.65 us (1%)
    pallas_call x1, Pallas kernels, body(): pl.pallas_call(functools.partial(kernel, wide, narrow), out_shape=(jax.Sh...  59 us
    unnamed x4, local copies, waits for them, and re-layouts  2.1 us

profile of v4, /device:TPU:1, one launch (start us, length us, event | category | flops | bytes accessed | tf_op | source)
XLA Modules:
  0.0 61.7 jit_solution(9867984367190789242)
XLA Ops:
  0.6 0.0 copy-start
  0.6 0.7 %copy-done = f32[3,192]{1,0:T(4,128)S(1)} copy-done((f32[3,192]{1,0:T(4,128)S(1)}, f32[3,192]{1,0:T(4,128)}, u32[]{:S(2)}) %copy-start) | copy-done | bytes 2328
  1.3 59.0 %shard_map.86 = (f32[5,3,8,1024]{3,2,1,0:T(8,128)S(1)}, f32[3,8,1024]{2,1,0:T(8,128)S(1)}) custom-call(f32[960,128]{1,0:T(8,128)} %bitcast.5, f32[3,192]{1,0:T(4,128)S(1)} %copy-done, bf16[1024,1024]{1,0:T(8,128)(2,1)} %constant.10.clone.fhigh_hbm, bf16[1024,1024]{1,0:T(8,128)(2,1)} %constant.11.clone.flow_hbm, bf16[1024,1024]{1,0:T(8,128)(2,1)} %constant.12.clone.ihigh_hbm, ...), custom_call_target="tpu_custom_call" | custom-call | tf_op jit(solution)/shard_map/pallas_call | solution.py:836
  60.3 0.8 %copy.11 = f32[5,3,8,1024]{3,2,1,0:T(8,128)} copy(f32[5,3,8,1024]{3,2,1,0:T(8,128)S(1)} %get-tuple-element.4) | data formatting | bytes 983040
  61.1 0.6 %copy.12 = f32[3,8,1024]{2,1,0:T(8,128)} copy(f32[3,8,1024]{2,1,0:T(8,128)S(1)} %get-tuple-element.5) | data formatting | bytes 196608
Async XLA Ops:
  0.6 0.7 %copy-start = (f32[3,192]{1,0:T(4,128)S(1)}, f32[3,192]{1,0:T(4,128)}, u32[]{:S(2)}) copy-start(f32[3,192]{1,0:T(4,128)} %bands_ref.1) | copy-start | bytes 6916
